TPU v7x, 128 devices: a whole 4x4x4 slice. The times are simulated.
128 devices in a mesh: fsdp: 16 (over z_hi, y, core), refresh: 8 (over z_lo, x).
Axes of the slice: x: 4, y: 4, z: 4 (z_hi: 2, z_lo: 2; z = z_hi * 2 + z_lo), core: 2. Of those that a mesh axis runs over, the one named last changes fastest.
Arguments:
- grad: bfloat16 [4096, 4096], P('fsdp', 'refresh'), may hold values from -6 to 6
- exp_avg: float32 [4096, 4096], P('fsdp', 'refresh'), may hold values from -1.75 to 1.75
- exp_avg_sq: float32 [4096, 4096], P('fsdp', 'refresh'), may hold values from 0.01 to 1
- left_codes: int32 [4096, 4096], P('fsdp'), may hold values from 0 to 15
- left_scales: float32 [4096, 32], P('fsdp'), may hold values from 0.001953125 to 0.005
- right_old_codes: int32 [4096, 4096], P('refresh'), may hold values from 0 to 15
- right_old_scales: float32 [4096, 32], P('refresh'), may hold values from 0.001953125 to 0.005
- right_new_codes: int32 [4096, 4096], P('refresh'), may hold values from 0 to 15
- right_new_scales: float32 [4096, 32], P('refresh'), may hold values from 0.001953125 to 0.005
Outputs:
- new_exp_avg: float32 [4096, 4096], P('fsdp', 'refresh')
- new_exp_avg_sq: float32 [4096, 4096], P('fsdp', 'refresh')
- update: float32 [4096, 4096], P('fsdp', 'refresh')
All inputs are finite; a program needn't handle non-finite values.
Results may differ from a plain program's by a relative error of at most 0.0054.
Values may be sent and summed in bfloat16 or wider, within the bound.
A program may use at most 128 MiB of HBM per device.

v0:
```python
import jax
import jax.numpy as jnp
from jax import lax
from jax.sharding import PartitionSpec as P

STEP = 20


first_beta = 0.9
second_beta = 0.95
epsilon = 1e-08


def dequantize(codes, scales):
    rows, columns = codes.shape
    groups = scales.shape[1]
    levels = codes.astype(jnp.float32) - 7.5
    scaled = levels.reshape(rows, groups, columns // groups) * scales[:, :, None]
    return scaled.reshape(rows, columns).astype(jnp.bfloat16)


def body(
    grad,
    exp_avg,
    exp_avg_sq,
    left_codes,
    left_scales,
    right_old_codes,
    right_old_scales,
    right_new_codes,
    right_new_scales,
):
    left_basis = dequantize(left_codes, left_scales)
    old_basis = dequantize(right_old_codes, right_old_scales)
    new_basis = dequantize(right_new_codes, right_new_scales)
    order = new_basis.shape[1]
    stripe = order // lax.axis_size("fsdp")
    offset = lax.axis_index("fsdp") * stripe
    new_stripe = lax.dynamic_slice_in_dim(new_basis, offset, stripe, 1)
    transition_term = jnp.einsum(
        "cj,ck->jk", old_basis, new_stripe, preferred_element_type=jnp.float32
    )
    grad_term = jnp.einsum("cj,ac->ja", new_basis, grad, preferred_element_type=jnp.float32)
    transition_tile, grad_right_wide = (
        lax.psum_scatter(transition_term, "refresh", scatter_dimension=0, tiled=True),
        lax.psum_scatter(grad_term, "refresh", scatter_dimension=0, tiled=True),
    )
    grad_right = grad_right_wide.astype(jnp.bfloat16)
    piece = lax.all_gather(transition_tile, "fsdp", axis=1, tiled=True)
    first_part = jnp.dot(exp_avg, piece, precision=lax.Precision.HIGHEST)
    second_part = jnp.dot(exp_avg_sq, piece * piece, precision=lax.Precision.HIGHEST)
    moment_terms = jnp.stack([first_part, second_part])
    moments = lax.psum_scatter(moment_terms, "refresh", scatter_dimension=2, tiled=True)
    first_moment = moments[0]
    second_moment = moments[1]
    columns = left_basis
    grad_rotated = lax.psum_scatter(
        jnp.einsum("ai,ja->ij", columns, grad_right, preferred_element_type=jnp.float32),
        "fsdp",
        scatter_dimension=0,
        tiled=True,
    )
    new_exp_avg = first_beta * first_moment + (1.0 - first_beta) * grad_rotated
    new_exp_avg_sq = second_beta * second_moment + (1.0 - second_beta) * grad_rotated * grad_rotated
    bias_first = 1.0 - first_beta**STEP
    bias_second = 1.0 - second_beta**STEP
    direction = (
        new_exp_avg / bias_first / (jnp.sqrt(new_exp_avg_sq / bias_second) + epsilon)
    ).astype(jnp.bfloat16)
    columns = left_basis
    partial_update = jnp.dot(
        columns,
        lax.all_gather(direction, "fsdp", axis=0, tiled=True),
        preferred_element_type=jnp.float32,
    ).astype(jnp.bfloat16)
    columns = new_basis
    update = jnp.einsum(
        "ak,ck->ac",
        lax.all_gather(partial_update, "refresh", axis=1, tiled=True),
        columns,
        preferred_element_type=jnp.float32,
    )
    return (new_exp_avg, new_exp_avg_sq, update)


def solution(mesh):
    return jax.shard_map(
        body,
        mesh=mesh,
        in_specs=(
            P("fsdp", "refresh"),
            P("fsdp", "refresh"),
            P("fsdp", "refresh"),
            P("fsdp", None),
            P("fsdp", None),
            P("refresh", None),
            P("refresh", None),
            P("refresh", None),
            P("refresh", None),
        ),
        out_specs=(P("fsdp", "refresh"), P("fsdp", "refresh"), P("fsdp", "refresh")),
        check_vma=False,
    )
```

profile of v0, /device:TPU:0, one launch (start us, length us, event | category | flops | bytes accessed | tf_op | source)
XLA Modules:
  0.0 550.7 jit_solution(13994211455597559278)
XLA Ops:
  7.2 1.0 copy.13
  8.2 1.0 copy.12
  9.2 5.5 %mul.75 = f32[512,32,128]{2,1,0:T(8,128)} broadcast(f32[512,32]{1,0:T(8,128)S(1)} %copy.13), dimensions={0,1} | broadcast | bytes 8454144 | tf_op jit(solution)/shard_map/mul | solution.py:18
  14.7 11.8 %fusion = bf16[512,4096]{1,0:T(8,128)(2,1)S(1)} fusion(f32[64,8,32,128]{3,2,1,0:T(8,128)} %bitcast.45, s32[512,4096]{1,0:T(8,128)} %param.16), kind=kLoop, calls=%fused_computation.1 | loop fusion | flops 8388608 | bytes 20971520 | tf_op jit(solution)/shard_map/convert_element_type | solution.py:19
  26.5 2.5 mul.72
  29.0 14.7 %fusion.7 = f32[4096,256]{1,0:T(8,128)} fusion(f32[64,8,32,128]{3,2,1,0:T(8,128)S(1)} %bitcast.44, s32[512,4096]{1,0:T(8,128)} %param.14, bf16[512,4096]{1,0:T(8,128)(2,1)S(1)} %fusion, s32[]{:T(128)S(6)} %select_n.3), kind=kOutput, calls=%fused_computation.9 | convolution fusion | flops 1082130432 | bytes 21233668 | tf_op jit(solution)/shard_map/cj,ck->jk/dot_general | solution.py:40
  43.7 0.0 reduce-scatter.9.cloned.1.call-start
  43.8 0.9 copy-done.5
  44.6 5.5 fusion.22
  50.2 49.3 %reduce-scatter.5.cloned.1.call-done = f32[512,256]{1,0:T(8,128)} async-done(((f32[4096,256]{1,0:T(8,128)}), f32[512,256]{1,0:T(8,128)}) %reduce-scatter.5.cloned.1.call-update) | async-done | bytes 524304 | tf_op jit(solution)/shard_map/reduce_scatter | solution.py:45
  99.5 0.4 reduce-scatter.11.cloned.1.call-start
  99.9 0.1 copy.14
  100.0 1.1 mul.83
  101.2 1.0 copy-done.3
  102.2 4.2 fusion.9
  106.4 47.4 %reduce-scatter.9.cloned.1.call-done = f32[512,256]{1,0:T(8,128)} async-done(((f32[4096,256]{1,0:T(8,128)}), f32[512,256]{1,0:T(8,128)}) %reduce-scatter.9.cloned.1.call-update) | async-done | bytes 524304 | tf_op jit(solution)/shard_map/reduce_scatter | solution.py:46
  153.8 5.5 %fusion.15 = f32[4096,512]{0,1:T(8,128)} fusion(bf16[256,4096]{1,0:T(8,128)(2,1)S(1)} %fusion.9, f32[512,256]{1,0:T(8,128)} %reduce-scatter.9.cloned.1.call-done), kind=kOutput, calls=%fused_computation.22 | convolution fusion | flops 1073872896 | bytes 11010048 | tf_op jit(solution)/shard_map/ai,ja->ij/dot_general | solution.py:58
  159.3 0.0 reduce-scatter.7.cloned.1.call-start
  159.4 75.7 %all-gather.4.cloned.1.call-done = f32[512,4096]{1,0:T(8,128)} async-done(((f32[512,256]{1,0:T(8,128)}), f32[512,4096]{1,0:T(8,128)}) %all-gather.4.cloned.1.call-update) | async-done | bytes 8388624 | tf_op jit(solution)/shard_map/all_gather | solution.py:49
  235.1 16.8 %convolution_bitcast_fusion = f32[1,256,4096]{1,2,0:T(8,128)S(1)} fusion(f32[512,4096]{1,0:T(8,128)} %all-gather.4.cloned.1.call-done, f32[256,512]{1,0:T(8,128)S(1)} %copy-done), kind=kOutput, calls=%fused_computation.8 | convolution fusion | flops 6442450944 | bytes 13107200 | tf_op jit(solution)/shard_map/dot_general | solution.py:50
  251.9 14.4 %fusion.4 = f32[1,256,4096]{1,2,0:T(8,128)S(1)} fusion(f32[256,512]{1,0:T(8,128)S(1)} %copy-done.4, f32[512,4096]{1,0:T(8,128)S(1)} %copy-done.1), kind=kOutput, calls=%fused_computation.7 | convolution fusion | flops 6444548096 | bytes 13107200 | tf_op jit(solution)/shard_map/dot_general | solution.py:51
  266.4 3.8 pad_maximum_fusion
  270.2 0.0 all-gather.6.cloned.1.call-start
  270.2 70.0 %reduce-scatter.11.cloned.1.call-done = f32[256,512]{0,1:T(8,128)} async-done(((f32[4096,512]{0,1:T(8,128)}), f32[256,512]{0,1:T(8,128)}) %reduce-scatter.11.cloned.1.call-update) | async-done | bytes 524304 | tf_op jit(solution)/shard_map/reduce_scatter | solution.py:57
  340.2 93.5 %reduce-scatter.7.cloned.1.call-done = f32[2,256,512]{1,2,0:T(8,128)} async-done(((f32[2,256,4096]{1,2,0:T(8,128)}), f32[2,256,512]{1,2,0:T(8,128)}) %reduce-scatter.7.cloned.1.call-update) | async-done | bytes 1048592 | tf_op jit(solution)/shard_map/reduce_scatter | solution.py:53
  433.8 2.6 divide_convert_fusion
  436.4 58.1 %all-gather.6.cloned.1.call-done = bf16[4096,512]{0,1:T(8,128)(2,1)} async-done(((bf16[256,512]{0,1:T(8,128)(2,1)}), bf16[4096,512]{0,1:T(8,128)(2,1)}) %all-gather.6.cloned.1.call-update) | async-done | bytes 4194320 | tf_op jit(solution)/shard_map/all_gather | solution.py:73
  494.5 4.2 convolution_convert_fusion
  498.7 2.0 copy.16
  500.8 1.0 copy.17
  501.8 37.0 %all-gather.8.cloned.1.call-done = bf16[256,4096]{1,0:T(8,128)(2,1)} async-done(((bf16[256,512]{1,0:T(8,128)(2,1)}), bf16[256,4096]{1,0:T(8,128)(2,1)}) %all-gather.8.cloned.1.call-update) | async-done | bytes 2097168 | tf_op jit(solution)/shard_map/all_gather | solution.py:79
  538.7 4.9 fusion.23
  (22 shorter events, 0.3 us)
Async XLA Ops:
  7.2 227.9 %copy-start = (f32[256,512]{1,0:T(8,128)S(1)}, f32[256,512]{1,0:T(8,128)}, u32[]{:S(2)}) copy-start(f32[256,512]{1,0:T(8,128)} %param.10) | copy-start | bytes 1572868
  7.2 92.3 %reduce-scatter.5.cloned.1.call-start = ((), (), s32[]{:S(2)}) async-start(), calls=%async_computation.4 | async-start | bytes 4718592 | tf_op jit(solution)/shard_map/reduce_scatter | solution.py:45
  26.5 2.5 copy-start.2
  43.7 0.9 copy-start.5
  43.7 110.0 %reduce-scatter.9.cloned.1.call-start = ((), (), s32[]{:S(2)}) async-start(), calls=%async_computation.7 | async-start | bytes 4718592 | tf_op jit(solution)/shard_map/reduce_scatter | solution.py:46
  50.1 49.8 %copy-start.6 = (f32[256,32]{0,1:T(8,128)S(1)}, f32[256,32]{0,1:T(8,128)}, u32[]{:S(2)}) copy-start(f32[256,32]{0,1:T(8,128)} %param.13) | copy-start | bytes 98308
  50.1 184.9 %all-gather.4.cloned.1.call-start = ((), (), s32[]{:S(2)}) async-start(), calls=%async_computation.5 | async-start | bytes 8912896 | tf_op jit(solution)/shard_map/all_gather | solution.py:49
  99.5 240.8 %reduce-scatter.11.cloned.1.call-start = ((), (), s32[]{:S(2)}) async-start(), calls=%async_computation.8 | async-start | bytes 8912896 | tf_op jit(solution)/shard_map/reduce_scatter | solution.py:57
  100.0 2.2 copy-start.3
  159.3 92.6 %copy-start.4 = (f32[256,512]{1,0:T(8,128)S(1)}, f32[256,512]{1,0:T(8,128)}, u32[]{:S(2)}) copy-start(f32[256,512]{1,0:T(8,128)} %param.11) | copy-start | bytes 1572868
  159.3 274.5 %reduce-scatter.7.cloned.1.call-start = ((), (), s32[]{:S(2)}) async-start(), calls=%async_computation.6 | async-start | bytes 9437184 | tf_op jit(solution)/shard_map/reduce_scatter | solution.py:53
  235.1 16.8 %copy-start.1 = (f32[512,4096]{1,0:T(8,128)S(1)}, f32[512,4096]{1,0:T(8,128)}, u32[]{:S(2)}) copy-start(f32[512,4096]{1,0:T(8,128)} %all-gather.4.cloned.1.call-done) | copy-start | bytes 25165828
  270.2 224.3 %all-gather.6.cloned.1.call-start = ((), (), s32[]{:S(2)}) async-start(), calls=%async_computation.9 | async-start | bytes 4456448 | tf_op jit(solution)/shard_map/all_gather | solution.py:73
  436.4 102.4 %all-gather.8.cloned.1.call-start = ((), (), s32[]{:S(2)}) async-start(), calls=%async_computation.10 | async-start | bytes 2359296 | tf_op jit(solution)/shard_map/all_gather | solution.py:79
Sparse Core Ops, SparseCore 0:
  43.8 55.5 reduce-scatter.4
  101.8 51.8 reduce-scatter.8
  156.0 78.9 all-gather.3
  239.2 100.9 reduce-scatter.10
  342.5 91.2 reduce-scatter.6
  436.5 57.9 all-gather.5
  498.9 39.8 all-gather.7
where the time goes:
time: 557 us; the launch traced here: 551 us
  waiting for transfers between devices  431 us (77%)
  matrix products  66 us (12%)
  other arithmetic  22.3 us (4%)
  local copies, waits for them, and re-layouts  16.2 us (3%)
  between operations  14.5 us (3%)
    reduce_scatter x1, waiting for transfers between devices, body(): lax.psum_scatter(moment_terms, 'refresh', scatter_dimension=2, tiled=True)  93.5 us
    all_gather x1, waiting for transfers between devices, body(): piece = lax.all_gather(transition_tile, 'fsdp', axis=1, tiled=True)  75.7 us
    reduce_scatter x1, waiting for transfers between devices, body(): lax.psum_scatter(jnp.einsum('ai,ja->ij', columns, grad_right, preferred_e...  70 us
    all_gather x1, waiting for transfers between devices, body(): lax.all_gather(direction, 'fsdp', axis=0, tiled=True)  58.1 us
    reduce_scatter x1, waiting for transfers between devices, body(): lax.psum_scatter(transition_term, 'refresh', scatter_dimension=0, tiled=T...  49.3 us
    reduce_scatter x1, waiting for transfers between devices, body(): lax.psum_scatter(grad_term, 'refresh', scatter_dimension=0, tiled=True)  47.4 us
    all_gather x1, waiting for transfers between devices, body(): lax.all_gather(partial_update, 'refresh', axis=1, tiled=True)  37 us
    dot_general x1, matrix products, body(): first_part = jnp.dot(exp_avg, piece, precision=lax.Precision.HIGHEST)  16.8 us
  transfers between devices with their start and end apart: 7, of which 7 were waited for; matrix products, arithmetic and copies ran while one was open for 10% of the time, Pallas kernels for 0%

commit v1 on v0

v1 whole, which is shorter than its diff:
```python
import jax
import jax.numpy as jnp
from jax import lax
from jax.experimental import pallas as pl
from jax.experimental.pallas import tpu as pltpu
from jax.sharding import PartitionSpec as P

STEP = 20
first_beta = 0.9
second_beta = 0.95
epsilon = 1e-08

N = 4096
FB = 256
RB = 512
NC = 4
CW = RB // NC
ROWS = 128
DEPTH = 3

BF = jnp.bfloat16
F32 = jnp.float32


def dot(a, b):
    return jnp.dot(a, b, preferred_element_type=F32)


class Wires:
    def __init__(self, send, recv):
        self.send, self.recv, self.count, self.out = send, recv, 0, []

    def copy(self, src, dst, device, landing):
        at = self.count
        self.count += 1

        def describe(a, b):
            return pltpu.make_async_remote_copy(
                src_ref=a,
                dst_ref=b,
                send_sem=self.send.at[at],
                recv_sem=self.recv.at[at],
                device_id=device,
                device_id_type=pl.DeviceIdType.MESH,
            )

        started = describe(src, dst)
        started.start()
        self.out.append(started)
        return describe(landing, landing).wait_recv

    def drain(self):
        for started in self.out:
            started.wait_send()


def kernel(
    grad, m1, m2, l_codes, l_scales, o_codes, o_scales, n_codes, n_scales,
    new_m1, new_m2, update,
    codes, o_slab, lb, nb, ob_t, tsend, town, trecv, tz_send, tz_recv, tf,
    mg, wcs, wcr, wown, wys, wyr, wsum, wzs, wzr, wb,
    gsend, gown, grecv, gz_send, gz_recv, mz_send, mz_recv, mown, df, pf,
    in_sem, o_sem, send_sem, recv_sem,
):
    f = lax.axis_index("fsdp")
    r = lax.axis_index("refresh")
    core, y, zh = lax.rem(f, 2), lax.rem(lax.div(f, 2), 4), lax.div(f, 8)
    x, zl = lax.rem(r, 4), lax.div(r, 4)

    def f_at(dz, dy, dc):
        zz = 1 - zh if dz else zh
        cc = 1 - core if dc else core
        return zz * 8 + lax.rem(y + dy + 4, 4) * 2 + cc

    def r_at(dz, dx):
        zz = 1 - zl if dz else zl
        return zz * 4 + lax.rem(x + dx + 4, 4)

    to_x = {d: (f, r_at(0, d)) for d in (1, 2, 3)}
    to_y = {d: (f_at(0, d, 0), r) for d in (1, 2, 3)}
    to_zl, to_zh, to_core = (f, r_at(1, 0)), (f_at(1, 0, 0), r), (f_at(0, 0, 1), r)
    wires = Wires(send_sem, recv_sem)

    jobs = [(n_codes, n_scales, nb, i) for i in range(2 * RB // (2 * ROWS))]
    jobs += [(l_codes, l_scales, lb, i) for i in range(FB // ROWS)]

    def fetch(job):
        src, _, _, i = jobs[job]
        return pltpu.make_async_copy(
            src.at[pl.ds(i * ROWS, ROWS), :], codes.at[job % DEPTH], in_sem.at[job % DEPTH]
        )

    o_in = [
        pltpu.make_async_copy(
            o_codes.at[:, pl.ds(pl.multiple_of(h * 2048 + f * 128, 128), 128)], o_slab.at[h], o_sem.at[h]
        )
        for h in range(2)
    ]
    for c in o_in:
        c.start()
    for job in range(DEPTH):
        fetch(job).start()

    barrier = pltpu.get_barrier_semaphore()
    friends = [*to_x.values(), *to_y.values(), to_zl, to_zh, to_core]
    for friend in friends:
        pl.semaphore_signal(barrier, inc=1, device_id=friend, device_id_type=pl.DeviceIdType.MESH)

    for h in range(2):
        o_in[h].wait()
        lanes = lax.broadcasted_iota(jnp.int32, (RB, 32), 1)
        scale = jnp.sum(jnp.where(lanes == f + 16 * h, o_scales[...], 0.0), axis=1, keepdims=True)
        values = (o_slab[h].astype(F32) - 7.5) * scale
        ob_t[pl.ds(h * 128, 128), :] = values.T.astype(BF)

    def expand(job):
        _, scales, out, i = jobs[job]
        fetch(job).wait()

        @pl.loop(0, ROWS // 32)
        def _(t):
            inner = pl.ds(pl.multiple_of(t * 32, 32), 32)
            outer = pl.ds(pl.multiple_of(i * ROWS + t * 32, 32), 32)
            s = scales[outer, :]
            for g in range(32):
                v = codes[job % DEPTH, inner, g * 128 : (g + 1) * 128].astype(F32) - 7.5
                out[outer, g * 128 : (g + 1) * 128] = (v * s[:, g : g + 1]).astype(BF)

        if job + DEPTH < len(jobs):
            fetch(job + DEPTH).start()

    for job in range(4):
        expand(job)

    for j in range(2):
        src = (m1, m2)[j]
        mg[pl.ds(x, 1), j] = src[...].astype(BF)[None]

    pl.semaphore_wait(barrier, len(friends))

    def columns(z, xx):
        return pl.ds(pl.multiple_of(z * 2048 + xx * RB, RB), RB)

    t_waits = []
    for d in (2, 1, 3):
        xx = lax.rem(x + d, 4)
        for z in range(2):
            tsend[d - 1, :, z * RB : (z + 1) * RB] = dot(ob_t[...], nb[:, columns(z, xx)]).astype(BF)
        t_waits.append(wires.copy(tsend.at[d - 1], trecv.at[d - 1], to_x[d], trecv.at[d - 1]))
    for z in range(2):
        town[:, z * RB : (z + 1) * RB] = dot(ob_t[...], nb[:, columns(z, x)])

    for job in range(4, len(jobs)):
        expand(job)

    def left_grad(block):
        lt = lb[:, pl.ds(pl.multiple_of(block * FB, FB), FB)]
        return lax.dot_general(lt, grad[...], (((0,), (0,)), ((), ())), preferred_element_type=F32)

    @pl.loop(0, 8)
    def _(q):
        wcs[q] = left_grad(lax.rem(q, 2) * 8 + lax.div(q, 2) * 2 + 1 - core).astype(BF)

    wc_wait = wires.copy(wcs, wcr, to_core, wcr)

    @pl.loop(0, 8)
    def _(q):
        wown[q] = left_grad(lax.rem(q, 2) * 8 + lax.div(q, 2) * 2 + core)

    wc_wait()
    wy_waits = []
    for d in (2, 1, 3):
        yy = lax.rem(y + d, 4)
        for z in range(2):
            wys[d - 1, z] = (wown[yy * 2 + z] + wcr[yy * 2 + z].astype(F32)).astype(BF)
        wy_waits.append(wires.copy(wys.at[d - 1], wyr.at[d - 1], to_y[d], wyr.at[d - 1]))
    for z in range(2):
        wsum[z] = wown[y * 2 + z] + wcr[y * 2 + z].astype(F32)

    for wait in t_waits:
        wait()
    m_waits = [
        wires.copy(mg.at[x], mg.at[x], to_x[d], mg.at[lax.rem(x + 4 - d, 4)]) for d in (2, 1, 3)
    ]

    def t_sum(z):
        rows = pl.ds(pl.multiple_of(z * 128, 128), 128)
        return (
            town[rows, :]
            + trecv[0, rows, :].astype(F32)
            + trecv[1, rows, :].astype(F32)
            + trecv[2, rows, :].astype(F32)
        )

    tz_send[...] = t_sum(1 - zl).astype(BF)
    tz_wait = wires.copy(tz_send, tz_recv, to_zl, tz_recv)
    tz_wait()
    tf[pl.ds(pl.multiple_of(f * 128, 128), 128), :] = (t_sum(zl) + tz_recv[...].astype(F32)).astype(BF)

    class Spread:
        def __init__(self, place):
            self.place = place
            own = place(f)
            self.a = {d: wires.copy(own, own, to_y[d], place(f_at(0, -d, 0))) for d in (2, 1, 3)}
            self.b = wires.copy(own, own, to_zh, place(f_at(1, 0, 0)))
            self.e = [wires.copy(own, own, to_core, place(f_at(0, 0, 1)))]

        def pass_core(self, dz, dy):
            block = self.place(f_at(dz, dy, 0))
            self.e.append(wires.copy(block, block, to_core, self.place(f_at(dz, dy, 1))))

        def pass_zh(self):
            self.b()
            block = self.place(f_at(1, 0, 0))
            self.c = {d: wires.copy(block, block, to_y[d], self.place(f_at(1, -d, 0))) for d in (2, 1, 3)}
            self.pass_core(1, 0)

        def pass_y(self):
            for d in (1, 3, 2):
                self.a[d]()
                self.pass_core(0, -d)
            for d in (1, 3, 2):
                self.c[d]()
                self.pass_core(1, -d)

        def finish(self):
            for wait in self.e:
                wait()

    spread_t = Spread(lambda i: tf.at[pl.ds(pl.multiple_of(i * 128, 128), 128), :])

    for wait in wy_waits:
        wait()

    def w_sum(z):
        return wsum[z] + wyr[0, z].astype(F32) + wyr[1, z].astype(F32) + wyr[2, z].astype(F32)

    wzs[...] = w_sum(1 - zh).astype(BF)
    wz_wait = wires.copy(wzs, wzr, to_zh, wzr)
    spread_t.pass_zh()
    wz_wait()
    wb[...] = (w_sum(zh) + wzr[...].astype(F32)).astype(BF)

    g_waits = []
    for d in (2, 1, 3):
        xx = lax.rem(x + d, 4)
        for z in range(2):
            gsend[d - 1, z] = dot(wb[...], nb[:, columns(z, xx)]).astype(BF)
        g_waits.append(wires.copy(gsend.at[d - 1], grecv.at[d - 1], to_x[d], grecv.at[d - 1]))
    for z in range(2):
        gown[z] = dot(wb[...], nb[:, columns(z, x)])

    spread_t.pass_y()
    spread_t.finish()
    for wait in m_waits:
        wait()

    half = 2 * CW

    def moments(z, c):
        cols = pl.ds(pl.multiple_of(z * RB + c * half, half), half)
        a = jnp.zeros((FB, half), F32)
        b = jnp.zeros((FB, half), F32)
        for k in range(4):
            t = tf[pl.ds(k * RB, RB), cols]
            a = a + dot(mg[k, 0], t)
            b = b + dot(mg[k, 1], t * t)
        return a, b

    mz_waits = []
    for c in range(2):
        a, b = moments(1 - zl, c)
        mz_send[c, 0] = a.astype(BF)
        mz_send[c, 1] = b.astype(BF)
        mz_waits.append(wires.copy(mz_send.at[c], mz_recv.at[c], to_zl, mz_recv.at[c]))

    for wait in g_waits:
        wait()

    def g_sum(z):
        return gown[z] + grecv[0, z].astype(F32) + grecv[1, z].astype(F32) + grecv[2, z].astype(F32)

    gz_send[...] = g_sum(1 - zl).astype(BF)
    gz_wait = wires.copy(gz_send, gz_recv, to_zl, gz_recv)
    for c in range(2):
        a, b = moments(zl, c)
        mown[c, 0] = a
        mown[c, 1] = b
    gz_wait()
    gown[pl.ds(zl, 1)] = (g_sum(zl) + gz_recv[...].astype(F32))[None]

    spreads = []
    for c in range(NC):
        h, off = (c * CW) // half, (c * CW) % half
        if off == 0:
            mz_waits[h]()
        cols = slice(c * CW, (c + 1) * CW)
        rot = gown[zl, :, cols]
        first = mown[h, 0, :, off : off + CW] + mz_recv[h, 0, :, off : off + CW].astype(F32)
        second = mown[h, 1, :, off : off + CW] + mz_recv[h, 1, :, off : off + CW].astype(F32)
        a = first_beta * first + (1.0 - first_beta) * rot
        b = second_beta * second + (1.0 - second_beta) * rot * rot
        new_m1[:, cols] = a
        new_m2[:, cols] = b
        bias_first = 1.0 - first_beta**STEP
        bias_second = 1.0 - second_beta**STEP
        direction = (a / bias_first) / (jnp.sqrt(b / bias_second) + epsilon)

        def place(i, c=c):
            return df.at[c, pl.ds(pl.multiple_of(i * FB, FB), FB), :]

        df[c, pl.ds(pl.multiple_of(f * FB, FB), FB), :] = direction.astype(BF)
        spreads.append(Spread(place))

    class Share:
        def __init__(self, place):
            self.place = place
            own = place(r)
            self.a = {d: wires.copy(own, own, to_x[d], place(r_at(0, -d))) for d in (2, 1, 3)}
            self.b = wires.copy(own, own, to_zl, place(r_at(1, 0)))

        def pass_zl(self):
            self.b()
            block = self.place(r_at(1, 0))
            self.c = {d: wires.copy(block, block, to_x[d], self.place(r_at(1, -d))) for d in (2, 1, 3)}

        def finish(self):
            for d in (1, 3, 2):
                self.a[d]()
            for d in (1, 3, 2):
                self.c[d]()

    shares = []
    for c in range(NC):
        spreads[c].pass_zh()
    for c in range(NC):
        spreads[c].pass_y()
        if c > 0:
            shares[c - 1].pass_zl()
        spreads[c].finish()
        pf[c, r] = dot(lb[...], df[c]).astype(BF)
        shares.append(Share(lambda i, c=c: pf.at[c, i]))
    shares[NC - 1].pass_zl()

    def update_part(c):
        total = jnp.zeros((FB, RB), F32)
        for i in range(8):
            n = nb[:, i * RB + c * CW : i * RB + (c + 1) * CW]
            total = total + lax.dot_general(pf[c, i], n, (((1,), (1,)), ((), ())), preferred_element_type=F32)
        return total

    for c in range(NC):
        shares[c].finish()
        if c == 0:
            update[...] = update_part(c)
        else:
            update[...] += update_part(c)
    wires.drain()


WIRES = 1 + 3 + 1 + 15 + 3 + 3 + 1 + 3 + 1 + 2 + NC * 22


def body(*args):
    vmem = pl.BlockSpec(memory_space=pltpu.VMEM)
    hbm = pl.BlockSpec(memory_space=pl.ANY)
    out = jax.ShapeDtypeStruct((FB, RB), F32)
    scratch = [
        pltpu.VMEM((DEPTH, ROWS, N), jnp.int32),
        pltpu.VMEM((2, RB, 128), jnp.int32),
        pltpu.VMEM((FB, N), BF),
        pltpu.VMEM((RB, N), BF),
        pltpu.VMEM((256, RB), BF),
        pltpu.VMEM((3, 256, 1024), BF),
        pltpu.VMEM((256, 1024), F32),
        pltpu.VMEM((3, 256, 1024), BF),
        pltpu.VMEM((128, 1024), BF),
        pltpu.VMEM((128, 1024), BF),
        pltpu.VMEM((2048, 1024), BF),
        pltpu.VMEM((4, 2, FB, RB), BF),
        pltpu.VMEM((8, FB, RB), BF),
        pltpu.VMEM((8, FB, RB), BF),
        pltpu.VMEM((8, FB, RB), F32),
        pltpu.VMEM((3, 2, FB, RB), BF),
        pltpu.VMEM((3, 2, FB, RB), BF),
        pltpu.VMEM((2, FB, RB), F32),
        pltpu.VMEM((FB, RB), BF),
        pltpu.VMEM((FB, RB), BF),
        pltpu.VMEM((FB, RB), BF),
        pltpu.VMEM((3, 2, FB, RB), BF),
        pltpu.VMEM((2, FB, RB), F32),
        pltpu.VMEM((3, 2, FB, RB), BF),
        pltpu.VMEM((FB, RB), BF),
        pltpu.VMEM((FB, RB), BF),
        pltpu.VMEM((2, 2, FB, RB // 2), BF),
        pltpu.VMEM((2, 2, FB, RB // 2), BF),
        pltpu.VMEM((2, 2, FB, RB // 2), F32),
        pltpu.VMEM((NC, N, CW), BF),
        pltpu.VMEM((NC, 8, FB, CW), BF),
        pltpu.SemaphoreType.DMA((DEPTH,)),
        pltpu.SemaphoreType.DMA((2,)),
        pltpu.SemaphoreType.DMA((WIRES,)),
        pltpu.SemaphoreType.DMA((WIRES,)),
    ]
    return pl.pallas_call(
        kernel,
        out_shape=(out, out, out),
        in_specs=[vmem, vmem, vmem, hbm, vmem, hbm, vmem, hbm, vmem],
        out_specs=(vmem, vmem, vmem),
        scratch_shapes=scratch,
        compiler_params=pltpu.CompilerParams(
            collective_id=0, has_side_effects=True, vmem_limit_bytes=62 * 2**20
        ),
    )(*args)


def solution(mesh):
    return jax.shard_map(
        body,
        mesh=mesh,
        in_specs=(
            P("fsdp", "refresh"),
            P("fsdp", "refresh"),
            P("fsdp", "refresh"),
            P("fsdp", None),
            P("fsdp", None),
            P("refresh", None),
            P("refresh", None),
            P("refresh", None),
            P("refresh", None),
        ),
        out_specs=(P("fsdp", "refresh"), P("fsdp", "refresh"), P("fsdp", "refresh")),
        check_vma=False,
    )
```

time: 557 us -> 153 us (0.27)
  waiting for transfers between devices: 431 us -> 0 us
  Pallas kernels: 0 us -> 141 us
  matrix products: 66 us -> 0 us
  other arithmetic: 22.3 us -> 0 us
  between operations: 14.5 us -> 0.64 us
  local copies, waits for them, and re-layouts: 16.2 us -> 10.5 us
    reduce_scatter x4 -> x0, waiting for transfers between devices: 260 us -> none  [the longest x1 93.5 us: body(): lax.psum_scatter(moment_terms, 'refresh', scatter_dimension=2, tiled=True)]
    all_gather x3 -> x0, waiting for transfers between devices: 171 us -> none  [the longest x1 75.7 us: body(): piece = lax.all_gather(transition_tile, 'fsdp', axis=1, tiled=True)]
    pallas_call x0 -> x1, Pallas kernels: none -> 141 us  [body(): pl.pallas_call(kernel, out_shape=(out, out, out), in_specs=[vmem, vmem, v...]
    dot_general x7 -> x0, matrix products: 66 us -> none  [the longest x1 16.8 us: body(): first_part = jnp.dot(exp_avg, piece, precision=lax.Precision.HIGHEST)]
    convert_element_type x3 -> x0, other arithmetic: 18.5 us -> none  [the longest x2 15.9 us: dequantize(): return scaled.reshape(rows, columns).astype(jnp.bfloat16)]
    mul x3 -> x0, local copies, waits for them, and re-layouts: 9.14 us -> none  [dequantize(): levels.reshape(rows, groups, columns // groups) * scales[:, :, None]]
  transfers between devices with their start and end apart: 7 -> 0, of which waited for: 7 -> 0; matrix products, arithmetic and copies ran while one was open for 10% -> 0% of each run, Pallas kernels for 0% -> 0%
where the time goes in v1:
time: 153 us; the launch traced here: 152 us
  Pallas kernels  141 us (92%)
  local copies, waits for them, and re-layouts  10.5 us (7%)
    pallas_call x1, Pallas kernels, body(): pl.pallas_call(kernel, out_shape=(out, out, out), in_specs=[vmem, vmem, v...  141 us
    unnamed x6, local copies, waits for them, and re-layouts  10.5 us

profile of v1, /device:TPU:0, one launch (start us, length us, event | category | flops | bytes accessed | tf_op | source)
XLA Modules:
  0.0 151.6 jit_solution(10121475748143623654)
XLA Ops:
  0.6 1.5 copy.12.l_scales
  2.1 1.7 %copy.13.o_scales = f32[512,32]{1,0:T(8,128)} copy(f32[512,32]{0,1:T(8,128)} %param.15) | data formatting | bytes 131072 | tf_op args[6]
  3.8 1.7 %copy.14.n_scales = f32[512,32]{1,0:T(8,128)} copy(f32[512,32]{0,1:T(8,128)} %param.17) | data formatting | bytes 131072 | tf_op args[8]
  5.5 140.5 %shard_map.112 = (f32[256,512]{1,0:T(8,128)}, f32[256,512]{1,0:T(8,128)}, f32[256,512]{1,0:T(8,128)}) custom-call(bf16[256,512]{1,0:T(8,128)(2,1)} %grad.1, f32[256,512]{1,0:T(8,128)} %m1.1, f32[256,512]{1,0:T(8,128)} %m2.1, s32[256,4096]{1,0:T(8,128)} %l_codes.1, f32[256,32]{1,0:T(8,128)} %copy.12.l_scales, s32[512,4096]{1,0:T(8,128)} %o_codes.1, ...), custom_call_target="tpu_custom_call" | custom-call | tf_op jit(solution)/shard_map/pallas_call | solution.py:405
  146.0 1.9 %copy.18 = f32[256,512]{1,0:T(8,128)} copy(f32[256,512]{1,0:T(8,128)} %get-tuple-element.6) | data formatting | bytes 1048576
  147.9 1.9 %copy.19 = f32[256,512]{1,0:T(8,128)} copy(f32[256,512]{1,0:T(8,128)} %get-tuple-element.7) | data formatting | bytes 1048576
  149.8 1.9 %copy.20 = f32[256,512]{1,0:T(8,128)} copy(f32[256,512]{1,0:T(8,128)} %get-tuple-element.8) | data formatting | bytes 1048576

commit v2 on v1

v2 whole, which is shorter than its diff:
```python
import jax
import jax.numpy as jnp
from jax import lax
from jax.experimental import pallas as pl
from jax.experimental.pallas import tpu as pltpu
from jax.sharding import PartitionSpec as P

STEP = 20
first_beta = 0.9
second_beta = 0.95
epsilon = 1e-08

N = 4096
FB = 256
RB = 512
HB = RB // 2
NC = 4
CW = RB // NC
N_DEPTH, L_DEPTH = 6, 4

BF = jnp.bfloat16
F32 = jnp.float32


def dot(a, b):
    return jnp.dot(a, b, preferred_element_type=F32)


class Wires:
    def __init__(self, send, recv):
        self.send, self.recv, self.count, self.out = send, recv, 0, []

    def copy(self, src, dst, device, landing):
        at = self.count
        self.count += 1

        def describe(a, b):
            return pltpu.make_async_remote_copy(
                src_ref=a,
                dst_ref=b,
                send_sem=self.send.at[at],
                recv_sem=self.recv.at[at],
                device_id=device,
                device_id_type=pl.DeviceIdType.MESH,
            )

        started = describe(src, dst)
        started.start()
        self.out.append(started)
        return describe(landing, landing).wait_recv

    def drain(self):
        for started in self.out:
            started.wait_send()


class Ring:
    def __init__(self, wires, place, half, at, to):
        self.wires, self.place, self.half, self.at, self.to = wires, place, half, at, to
        own = place(at(0))
        self.up = wires.copy(own, own, to[1], place(at(-1)))
        self.down = wires.copy(own, own, to[3], place(at(1)))

    def forward(self):
        far = self.place(self.at(2))
        self.up()
        piece = self.half(self.place(self.at(-1)), 0)
        self.far_up = self.wires.copy(piece, piece, self.to[1], self.half(far, 0))
        self.down()
        piece = self.half(self.place(self.at(1)), 1)
        self.far_down = self.wires.copy(piece, piece, self.to[3], self.half(far, 1))

    def finish(self):
        self.far_up()
        self.far_down()


def kernel(
    grad, m1, m2, l_codes, l_scales, o_codes, o_scales, n_codes, n_scales,
    new_m1, new_m2, update,
    ncode, lcode, o_slab, lb, nb, n2, ob_t, tsend, town, trecv, tz_send, tz_recv, tf,
    mg, wcs, wcr, wys, wyr, wsum, wzs, wzr, wb, w2,
    gsend, gown, grecv, mz_send, mz_recv, mown, df, pf,
    n_sem, l_sem, o_sem, send_sem, recv_sem,
):
    f = lax.axis_index("fsdp")
    r = lax.axis_index("refresh")
    core, y, zh = lax.rem(f, 2), lax.rem(lax.div(f, 2), 4), lax.div(f, 8)
    x, zl = lax.rem(r, 4), lax.div(r, 4)

    def f_at(dz, dy, dc):
        zz = 1 - zh if dz else zh
        cc = 1 - core if dc else core
        return zz * 8 + lax.rem(y + dy + 4, 4) * 2 + cc

    def r_at(dz, dx):
        zz = 1 - zl if dz else zl
        return zz * 4 + lax.rem(x + dx + 4, 4)

    to_x = {d: (f, r_at(0, d)) for d in (1, 2, 3)}
    to_y = {d: (f_at(0, d, 0), r) for d in (1, 2, 3)}
    to_zl, to_zh, to_core = (f, r_at(1, 0)), (f_at(1, 0, 0), r), (f_at(0, 0, 1), r)
    wires = Wires(send_sem, recv_sem)

    def offset(v, unit):
        return pl.multiple_of(v, unit)

    n_jobs = [(z * 2048 + lax.rem(x + d, 4) * RB + h * HB) for h in range(2) for d in (2, 1, 3, 0) for z in range(2)]
    l_jobs = [(z * 2048 + lax.rem(y + d, 4) * RB) for d in (2, 1, 3, 0) for z in range(2)]

    def n_fetch(job):
        return pltpu.make_async_copy(
            n_codes.at[:, pl.ds(offset(n_jobs[job], HB), HB)], ncode.at[job % N_DEPTH], n_sem.at[job % N_DEPTH]
        )

    def l_fetch(job):
        return pltpu.make_async_copy(
            l_codes.at[:, pl.ds(offset(l_jobs[job], RB), RB)], lcode.at[job % L_DEPTH], l_sem.at[job % L_DEPTH]
        )

    o_in = [
        pltpu.make_async_copy(o_codes.at[:, pl.ds(offset(h * 2048 + f * 128, 128), 128)], o_slab.at[h], o_sem.at[h])
        for h in range(2)
    ]
    for c in o_in:
        c.start()
    for job in range(N_DEPTH):
        n_fetch(job).start()
    for job in range(L_DEPTH):
        l_fetch(job).start()

    barrier = pltpu.get_barrier_semaphore()
    friends = [*to_x.values(), *to_y.values(), to_zl, to_zh, to_core]
    for friend in friends:
        pl.semaphore_signal(barrier, inc=1, device_id=friend, device_id_type=pl.DeviceIdType.MESH)

    def widened(scales, group, rows):
        eight = scales[pl.ds(offset(lax.div(group, 8) * 8, 8), 8), rows * 128 : (rows + 1) * 128]
        chosen = lax.broadcasted_iota(jnp.int32, (8, 128), 0) == lax.rem(group, 8)
        row = jnp.sum(jnp.where(chosen, eight, 0.0), axis=0, keepdims=True)
        return jnp.broadcast_to(row, (128, 128)).T

    for h in range(2):
        o_in[h].wait()
        for b in range(4):
            values = (o_slab[h, b * 128 : (b + 1) * 128, :].astype(F32) - 7.5) * widened(o_scales, f + 16 * h, b)
            ob_t[h * 128 : (h + 1) * 128, b * 128 : (b + 1) * 128] = values.T.astype(BF)

    for j in range(2):
        mg[pl.ds(x, 1), j] = (m1, m2)[j][...].astype(BF)[None]

    def expand(slot, scales, out, column, rows, groups):
        for g in range(groups):
            for b in range(rows // 128):
                part = slice(b * 128, (b + 1) * 128)
                v = slot[part, g * 128 : (g + 1) * 128].astype(F32) - 7.5
                v = v * widened(scales, lax.div(column, 128) + g, b)
                out[part, pl.ds(offset(column + g * 128, 128), 128)] = v.astype(BF)

    def n_expand(job):
        n_fetch(job).wait()
        expand(ncode.at[job % N_DEPTH], n_scales, nb, n_jobs[job], RB, 2)
        if job + N_DEPTH < len(n_jobs):
            n_fetch(job + N_DEPTH).start()

    def l_expand(job):
        l_fetch(job).wait()
        expand(lcode.at[job % L_DEPTH], l_scales, lb, l_jobs[job], FB, 4)
        if job + L_DEPTH < len(l_jobs):
            l_fetch(job + L_DEPTH).start()

    t_waits = [[], []]
    for h in range(2):
        for i, d in enumerate((2, 1, 3, 0)):
            for z in range(2):
                job = (h * 4 + i) * 2 + z
                n_expand(job)
                part = dot(ob_t[...], nb[:, pl.ds(offset(n_jobs[job], HB), HB)])
                cols = slice(z * HB, (z + 1) * HB)
                if d:
                    tsend[h, d - 1, :, cols] = part.astype(BF)
                else:
                    town[h, :, cols] = part
            if h == 0 and i == 0:
                pl.semaphore_wait(barrier, len(friends))
            if d:
                t_waits[h].append(wires.copy(tsend.at[h, d - 1], trecv.at[h, d - 1], to_x[d], trecv.at[h, d - 1]))

    mine = pl.ds(offset(core * 256, 256), 256)
    theirs = pl.ds(offset((1 - core) * 256, 256), 256)
    n_wait = wires.copy(
        nb.at[mine, pl.ds(offset((1 - zl) * 2048, 2048), 2048)], n2.at[mine, :], to_zl, n2.at[mine, :]
    )

    def left_grad(z, d, c):
        lt = lb[:, pl.ds(offset(z * 2048 + lax.rem(y + d, 4) * RB + c * FB, FB), FB)]
        return lax.dot_general(lt, grad[...], (((0,), (0,)), ((), ())), preferred_element_type=F32)

    wc_waits, wy_waits = {}, []

    def send_w(d):
        parts = [left_grad(z, d, core) for z in range(2)]
        wc_waits[d]()
        for z in range(2):
            total = parts[z] + wcr[d, z].astype(F32)
            if d:
                wys[d - 1, z] = total.astype(BF)
            else:
                wsum[z] = total
        if d:
            wy_waits.append(wires.copy(wys.at[d - 1], wyr.at[d - 1], to_y[d], wyr.at[d - 1]))

    before = None
    for i, d in enumerate((2, 1, 3, 0)):
        for z in range(2):
            l_expand(2 * i + z)
            wcs[d, z] = left_grad(z, d, 1 - core).astype(BF)
        wc_waits[d] = wires.copy(wcs.at[d], wcr.at[d], to_core, wcr.at[d])
        if before is not None:
            send_w(before)
        before = d
    send_w(before)

    def t_sum(h, z):
        rows = pl.ds(offset(z * 128, 128), 128)
        total = town[h, rows, :]
        for k in range(3):
            total = total + trecv[h, k, rows, :].astype(F32)
        return total

    def t_swap(h):
        for wait in t_waits[h]:
            wait()
        tz_send[h] = t_sum(h, 1 - zl).astype(BF)
        return wires.copy(tz_send.at[h], tz_recv.at[h], to_zl, tz_recv.at[h])

    def t_place(h):
        return lambda i: tf.at[h, pl.ds(offset(i * 128, 128), 128), :]

    def t_own(h):
        tf[h, pl.ds(offset(f * 128, 128), 128), :] = (t_sum(h, zl) + tz_recv[h].astype(F32)).astype(BF)

    def half_of(rows):
        return lambda block, k: block.at[pl.ds(k * rows, rows), :]

    class Spread:
        def __init__(self, place, rows):
            self.place, self.half = place, half_of(rows // 2)
            own = place(f)
            self.z = wires.copy(own, own, to_zh, place(f_at(1, 0, 0)))
            self.e = [wires.copy(own, own, to_core, place(f_at(0, 0, 1)))]

        def pass_core(self, dz, dy):
            block = self.place(f_at(dz, dy, 0))
            self.e.append(wires.copy(block, block, to_core, self.place(f_at(dz, dy, 1))))

        def start(self):
            self.near = Ring(wires, self.place, self.half, lambda d: f_at(0, d, 0), to_y)
            self.z()
            self.other = Ring(wires, self.place, self.half, lambda d: f_at(1, d, 0), to_y)
            self.pass_core(1, 0)

        def forward(self):
            for dz, ring in enumerate((self.near, self.other)):
                ring.forward()
                self.pass_core(dz, 1)
                self.pass_core(dz, -1)

        def finish(self):
            for dz, ring in enumerate((self.near, self.other)):
                ring.finish()
                self.pass_core(dz, 2)
            for wait in self.e:
                wait()

    tz_wait = t_swap(0)
    tz_wait()
    t_own(0)
    spread_t = [Spread(t_place(0), 128)]
    spread_t[0].start()
    tz_wait = t_swap(1)
    ring_m = Ring(wires, lambda i: mg.at[i], lambda block, k: block.at[k], lambda d: lax.rem(x + d + 4, 4), to_x)
    n_wait()
    n_core_wait = wires.copy(n2.at[mine, :], n2.at[mine, :], to_core, n2.at[theirs, :])
    tz_wait()
    t_own(1)
    spread_t.append(Spread(t_place(1), 128))
    spread_t[0].forward()

    for wait in wy_waits:
        wait()

    def w_sum(z):
        total = wsum[z]
        for k in range(3):
            total = total + wyr[k, z].astype(F32)
        return total

    wzs[...] = w_sum(1 - zh).astype(BF)
    wz_wait = wires.copy(wzs, wzr, to_zh, wzr)
    spread_t[1].start()
    wz_wait()
    wb[...] = (w_sum(zh) + wzr[...].astype(F32)).astype(BF)
    w2_wait = wires.copy(wb, w2, to_zl, w2)
    ring_m.forward()
    spread_t[0].finish()
    w2_wait()
    n_core_wait()

    def rotated(d):
        xx = lax.rem(x + d, 4)
        here = dot(wb[...], nb[:, pl.ds(offset(zl * 2048 + xx * RB, RB), RB)])
        return here + dot(w2[...], n2[:, pl.ds(offset(xx * RB, RB), RB)])

    g_waits = []
    for d in (2, 1, 3):
        gsend[d - 1] = rotated(d).astype(BF)
        g_waits.append(wires.copy(gsend.at[d - 1], grecv.at[d - 1], to_x[d], grecv.at[d - 1]))
    gown[...] = rotated(0)

    def moments(z, h):
        a = jnp.zeros((FB, HB), F32)
        b = jnp.zeros((FB, HB), F32)
        for k in range(4):
            t = tf[h, pl.ds(k * RB, RB), pl.ds(offset(z * HB, HB), HB)]
            a = a + dot(mg[k, 0], t)
            b = b + dot(mg[k, 1], t * t)
        return a, b

    def m_swap(h):
        a, b = moments(1 - zl, h)
        mz_send[h, 0] = a.astype(BF)
        mz_send[h, 1] = b.astype(BF)
        return wires.copy(mz_send.at[h], mz_recv.at[h], to_zl, mz_recv.at[h])

    spread_t[1].forward()
    ring_m.finish()
    mz_waits = [m_swap(0)]
    mown[0, 0], mown[0, 1] = moments(zl, 0)
    spread_t[1].finish()
    mz_waits.append(m_swap(1))
    mown[1, 0], mown[1, 1] = moments(zl, 1)
    for wait in g_waits:
        wait()

    spreads = []
    for c in range(NC):
        h, off = (c * CW) // HB, (c * CW) % HB
        if off == 0:
            mz_waits[h]()
        cols = slice(c * CW, (c + 1) * CW)
        rot = gown[:, cols]
        for k in range(3):
            rot = rot + grecv[k, :, cols].astype(F32)
        first = mown[h, 0, :, off : off + CW] + mz_recv[h, 0, :, off : off + CW].astype(F32)
        second = mown[h, 1, :, off : off + CW] + mz_recv[h, 1, :, off : off + CW].astype(F32)
        a = first_beta * first + (1.0 - first_beta) * rot
        b = second_beta * second + (1.0 - second_beta) * rot * rot
        new_m1[:, cols] = a
        new_m2[:, cols] = b
        bias_first = 1.0 - first_beta**STEP
        bias_second = 1.0 - second_beta**STEP
        direction = (a / bias_first) / (jnp.sqrt(b / bias_second) + epsilon)

        def place(i, c=c):
            return df.at[c, pl.ds(offset(i * FB, FB), FB), :]

        df[c, pl.ds(offset(f * FB, FB), FB), :] = direction.astype(BF)
        spreads.append(Spread(place, FB))

    class Share:
        def __init__(self, place):
            self.place = place
            own = place(r)
            self.z = wires.copy(own, own, to_zl, place(r_at(1, 0)))
            self.near = Ring(wires, place, half_of(FB // 2), lambda d: r_at(0, d), to_x)

        def start(self):
            self.z()
            self.other = Ring(wires, self.place, half_of(FB // 2), lambda d: r_at(1, d), to_x)

        def forward(self):
            self.near.forward()
            self.other.forward()

        def finish(self):
            self.near.finish()
            self.other.finish()

    def update_part(c):
        total = jnp.zeros((FB, RB), F32)
        for i in range(8):
            n = nb[:, i * RB + c * CW : i * RB + (c + 1) * CW]
            total = total + lax.dot_general(pf[c, i], n, (((1,), (1,)), ((), ())), preferred_element_type=F32)
        if c == 0:
            update[...] = total
        else:
            update[...] += total

    shares = []
    spreads[0].start()
    for c in range(NC):
        if c + 1 < NC:
            spreads[c + 1].start()
        spreads[c].forward()
        if c >= 1:
            shares[c - 1].start()
        spreads[c].finish()
        pf[c, r] = dot(lb[...], df[c]).astype(BF)
        shares.append(Share(lambda i, c=c: pf.at[c, i]))
        if c >= 1:
            shares[c - 1].forward()
        if c >= 2:
            shares[c - 2].finish()
            update_part(c - 2)
    shares[NC - 1].start()
    shares[NC - 2].finish()
    update_part(NC - 2)
    shares[NC - 1].forward()
    shares[NC - 1].finish()
    update_part(NC - 1)
    wires.drain()


WIRES = 6 + 2 + 4 + 3 + 2 + 2 + 2 * 17 + 4 + 3 + 2 + NC * (17 + 9)


def hand_over(*refs):
    for given, result in zip(refs[:3], refs[3:]):
        result[...] = given[...]


def body(
    grad, exp_avg, exp_avg_sq, left_codes, left_scales,
    right_old_codes, right_old_scales, right_new_codes, right_new_scales,
):
    vmem = pl.BlockSpec(memory_space=pltpu.VMEM)
    hbm = pl.BlockSpec(memory_space=pl.ANY)
    out = jax.ShapeDtypeStruct((FB, RB), F32)
    scratch = [
        pltpu.VMEM((N_DEPTH, RB, HB), jnp.int32),
        pltpu.VMEM((L_DEPTH, FB, RB), jnp.int32),
        pltpu.VMEM((2, RB, 128), jnp.int32),
        pltpu.VMEM((FB, N), BF),
        pltpu.VMEM((RB, N), BF),
        pltpu.VMEM((RB, N // 2), BF),
        pltpu.VMEM((256, RB), BF),
        pltpu.VMEM((2, 3, 256, RB), BF),
        pltpu.VMEM((2, 256, RB), F32),
        pltpu.VMEM((2, 3, 256, RB), BF),
        pltpu.VMEM((2, 128, RB), BF),
        pltpu.VMEM((2, 128, RB), BF),
        pltpu.VMEM((2, N // 2, RB), BF),
        pltpu.VMEM((4, 2, FB, RB), BF),
        pltpu.VMEM((4, 2, FB, RB), BF),
        pltpu.VMEM((4, 2, FB, RB), BF),
        pltpu.VMEM((3, 2, FB, RB), BF),
        pltpu.VMEM((3, 2, FB, RB), BF),
        pltpu.VMEM((2, FB, RB), F32),
        pltpu.VMEM((FB, RB), BF),
        pltpu.VMEM((FB, RB), BF),
        pltpu.VMEM((FB, RB), BF),
        pltpu.VMEM((FB, RB), BF),
        pltpu.VMEM((3, FB, RB), BF),
        pltpu.VMEM((FB, RB), F32),
        pltpu.VMEM((3, FB, RB), BF),
        pltpu.VMEM((2, 2, FB, HB), BF),
        pltpu.VMEM((2, 2, FB, HB), BF),
        pltpu.VMEM((2, 2, FB, HB), F32),
        pltpu.VMEM((NC, N, CW), BF),
        pltpu.VMEM((NC, 8, FB, CW), BF),
        pltpu.SemaphoreType.DMA((N_DEPTH,)),
        pltpu.SemaphoreType.DMA((L_DEPTH,)),
        pltpu.SemaphoreType.DMA((2,)),
        pltpu.SemaphoreType.DMA((WIRES,)),
        pltpu.SemaphoreType.DMA((WIRES,)),
    ]
    results = pl.pallas_call(
        kernel,
        out_shape=(out, out, out),
        in_specs=[vmem, vmem, vmem, hbm, vmem, hbm, vmem, hbm, vmem],
        out_specs=(vmem, vmem, vmem),
        scratch_shapes=scratch,
        compiler_params=pltpu.CompilerParams(
            collective_id=0, has_side_effects=True, vmem_limit_bytes=62 * 2**20
        ),
    )(
        grad, exp_avg, exp_avg_sq, left_codes, left_scales.T,
        right_old_codes, right_old_scales.T, right_new_codes, right_new_scales.T,
    )
    return pl.pallas_call(
        hand_over,
        out_shape=(out, out, out),
        in_specs=[vmem] * 3,
        out_specs=(vmem,) * 3,
    )(*results)


def solution(mesh):
    return jax.shard_map(
        body,
        mesh=mesh,
        in_specs=(
            P("fsdp", "refresh"),
            P("fsdp", "refresh"),
            P("fsdp", "refresh"),
            P("fsdp", None),
            P("fsdp", None),
            P("refresh", None),
            P("refresh", None),
            P("refresh", None),
            P("refresh", None),
        ),
        out_specs=(P("fsdp", "refresh"), P("fsdp", "refresh"), P("fsdp", "refresh")),
        check_vma=False,
    )
```

time: 153 us -> 142 us (0.928)
  local copies, waits for them, and re-layouts: 10.5 us -> 0 us
    unnamed x6 -> x0, local copies, waits for them, and re-layouts: 10.5 us -> none
    pallas_call x0 -> x1, Pallas kernels: none -> 2.53 us  [body(): pl.pallas_call(hand_over, out_shape=(out, out, out), in_specs=[vmem] * 3,...]
    pallas_call x1, Pallas kernels: 141 us -> 138 us  [body(): pl.pallas_call(kernel, out_shape=(out, out, out), in_specs=[vmem, vmem, v...]
where the time goes in v2:
time: 142 us; the launch traced here: 141 us
  Pallas kernels  141 us (99%)
    pallas_call x1, Pallas kernels, body(): pl.pallas_call(kernel, out_shape=(out, out, out), in_specs=[vmem, vmem, v...  138 us

profile of v2, /device:TPU:0, one launch (start us, length us, event | category | flops | bytes accessed | tf_op | source)
XLA Modules:
  0.0 141.4 jit_solution(3595300951300983466)
XLA Ops:
  0.6 138.2 %shard_map.112 = (f32[256,512]{1,0:T(8,128)}, f32[256,512]{1,0:T(8,128)}, f32[256,512]{1,0:T(8,128)}) custom-call(bf16[256,512]{1,0:T(8,128)(2,1)} %grad.1, f32[256,512]{1,0:T(8,128)} %m1.1, f32[256,512]{1,0:T(8,128)} %m2.1, s32[256,4096]{1,0:T(8,128)} %l_codes.1, f32[32,256]{1,0:T(8,128)} %bitcast.5, s32[512,4096]{1,0:T(8,128)} %o_codes.1, ...), custom_call_target="tpu_custom_call" | custom-call | tf_op jit(solution)/shard_map/pallas_call | solution.py:478
  138.9 2.5 %shard_map.113 = (f32[256,512]{1,0:T(8,128)}, f32[256,512]{1,0:T(8,128)}, f32[256,512]{1,0:T(8,128)}) custom-call(f32[256,512]{1,0:T(8,128)} %get-tuple-element.6.refs_0_, f32[256,512]{1,0:T(8,128)} %get-tuple-element.7.refs_1_, f32[256,512]{1,0:T(8,128)} %get-tuple-element.8.refs_2_), custom_call_target="tpu_custom_call" | custom-call | tf_op jit(solution)/shard_map/pallas_call | solution.py:491

commit v3 on v2

--- a/solution.py
+++ b/solution.py
@@ -169,8 +169,19 @@
         if job + L_DEPTH < len(l_jobs):
             l_fetch(job + L_DEPTH).start()
 
+    mine = pl.ds(offset(core * 256, 256), 256)
+    theirs = pl.ds(offset((1 - core) * 256, 256), 256)
+    n_waits = []
+
+    def n_swap(h, d):
+        within = lax.rem(x + d, 4) * RB + h * HB
+        landing = n2.at[mine, pl.ds(offset(within, HB), HB)]
+        src = nb.at[mine, pl.ds(offset((1 - zl) * 2048 + within, HB), HB)]
+        n_waits.append(wires.copy(src, landing, to_zl, landing))
+
     t_waits = [[], []]
-    for h in range(2):
+
+    def t_part(h):
         for i, d in enumerate((2, 1, 3, 0)):
             for z in range(2):
                 job = (h * 4 + i) * 2 + z
@@ -185,12 +196,9 @@
                 pl.semaphore_wait(barrier, len(friends))
             if d:
                 t_waits[h].append(wires.copy(tsend.at[h, d - 1], trecv.at[h, d - 1], to_x[d], trecv.at[h, d - 1]))
-
-    mine = pl.ds(offset(core * 256, 256), 256)
-    theirs = pl.ds(offset((1 - core) * 256, 256), 256)
-    n_wait = wires.copy(
-        nb.at[mine, pl.ds(offset((1 - zl) * 2048, 2048), 2048)], n2.at[mine, :], to_zl, n2.at[mine, :]
-    )
+            n_swap(h, d)
+
+    t_part(0)
 
     def left_grad(z, d, c):
         lt = lb[:, pl.ds(offset(z * 2048 + lax.rem(y + d, 4) * RB + c * FB, FB), FB)]
@@ -221,6 +229,9 @@
         before = d
     send_w(before)
 
+    t_part(1)
+
+
     def t_sum(h, z):
         rows = pl.ds(offset(z * 128, 128), 128)
         total = town[h, rows, :]
@@ -280,15 +291,6 @@
     spread_t[0].start()
     tz_wait = t_swap(1)
     ring_m = Ring(wires, lambda i: mg.at[i], lambda block, k: block.at[k], lambda d: lax.rem(x + d + 4, 4), to_x)
-    n_wait()
-    n_core_wait = wires.copy(n2.at[mine, :], n2.at[mine, :], to_core, n2.at[theirs, :])
-    tz_wait()
-    t_own(1)
-    spread_t.append(Spread(t_place(1), 128))
-    spread_t[0].forward()
-
-    for wait in wy_waits:
-        wait()
 
     def w_sum(z):
         total = wsum[z]
@@ -296,14 +298,23 @@
             total = total + wyr[k, z].astype(F32)
         return total
 
+    for wait in wy_waits:
+        wait()
     wzs[...] = w_sum(1 - zh).astype(BF)
     wz_wait = wires.copy(wzs, wzr, to_zh, wzr)
-    spread_t[1].start()
+    tz_wait()
+    t_own(1)
+    spread_t.append(Spread(t_place(1), 128))
+    spread_t[0].forward()
     wz_wait()
     wb[...] = (w_sum(zh) + wzr[...].astype(F32)).astype(BF)
     w2_wait = wires.copy(wb, w2, to_zl, w2)
+    spread_t[1].start()
+    for wait in n_waits:
+        wait()
+    n_core_wait = wires.copy(n2.at[mine, :], n2.at[mine, :], to_core, n2.at[theirs, :])
+    spread_t[0].finish()
     ring_m.forward()
-    spread_t[0].finish()
     w2_wait()
     n_core_wait()
 
@@ -399,10 +410,13 @@
 
     shares = []
     spreads[0].start()
+    spreads[1].start()
+    spreads[0].forward()
     for c in range(NC):
+        if c + 2 < NC:
+            spreads[c + 2].start()
         if c + 1 < NC:
-            spreads[c + 1].start()
-        spreads[c].forward()
+            spreads[c + 1].forward()
         if c >= 1:
             shares[c - 1].start()
         spreads[c].finish()
@@ -422,7 +436,7 @@
     wires.drain()
 
 
-WIRES = 6 + 2 + 4 + 3 + 2 + 2 + 2 * 17 + 4 + 3 + 2 + NC * (17 + 9)
+WIRES = 6 + 9 + 4 + 3 + 2 + 2 + 2 * 17 + 4 + 3 + 2 + NC * (17 + 9)
 
 
 def hand_over(*refs):

time: 142 us -> 131 us (0.923)
  Pallas kernels: 141 us -> 130 us
    pallas_call x1, Pallas kernels: 138 us -> 128 us  [body(): pl.pallas_call(kernel, out_shape=(out, out, out), in_specs=[vmem, vmem, v...]
where the time goes in v3:
time: 131 us
  Pallas kernels  130 us (99%)
    pallas_call x1, Pallas kernels, body(): pl.pallas_call(kernel, out_shape=(out, out, out), in_specs=[vmem, vmem, v...  128 us

profile of v3, /device:TPU:0, one launch (start us, length us, event | category | flops | bytes accessed | tf_op | source)
XLA Modules:
  0.0 131.0 jit_solution(9471940765066296653)
XLA Ops:
  0.6 127.8 %shard_map.112 = (f32[256,512]{1,0:T(8,128)}, f32[256,512]{1,0:T(8,128)}, f32[256,512]{1,0:T(8,128)}) custom-call(bf16[256,512]{1,0:T(8,128)(2,1)} %grad.1, f32[256,512]{1,0:T(8,128)} %m1.1, f32[256,512]{1,0:T(8,128)} %m2.1, s32[256,4096]{1,0:T(8,128)} %l_codes.1, f32[32,256]{1,0:T(8,128)} %bitcast.5, s32[512,4096]{1,0:T(8,128)} %o_codes.1, ...), custom_call_target="tpu_custom_call" | custom-call | tf_op jit(solution)/shard_map/pallas_call | solution.py:492
  128.4 2.5 %shard_map.113 = (f32[256,512]{1,0:T(8,128)}, f32[256,512]{1,0:T(8,128)}, f32[256,512]{1,0:T(8,128)}) custom-call(f32[256,512]{1,0:T(8,128)} %get-tuple-element.6.refs_0_, f32[256,512]{1,0:T(8,128)} %get-tuple-element.7.refs_1_, f32[256,512]{1,0:T(8,128)} %get-tuple-element.8.refs_2_), custom_call_target="tpu_custom_call" | custom-call | tf_op jit(solution)/shard_map/pallas_call | solution.py:505

commit v4 on v3

--- a/solution.py
+++ b/solution.py
@@ -289,8 +289,8 @@
     t_own(0)
     spread_t = [Spread(t_place(0), 128)]
     spread_t[0].start()
+    ring_m = Ring(wires, lambda i: mg.at[i], lambda block, k: block.at[k], lambda d: lax.rem(x + d + 4, 4), to_x)
     tz_wait = t_swap(1)
-    ring_m = Ring(wires, lambda i: mg.at[i], lambda block, k: block.at[k], lambda d: lax.rem(x + d + 4, 4), to_x)
 
     def w_sum(z):
         total = wsum[z]
@@ -315,6 +315,7 @@
     n_core_wait = wires.copy(n2.at[mine, :], n2.at[mine, :], to_core, n2.at[theirs, :])
     spread_t[0].finish()
     ring_m.forward()
+    spread_t[1].forward()
     w2_wait()
     n_core_wait()
 
@@ -344,7 +345,6 @@
         mz_send[h, 1] = b.astype(BF)
         return wires.copy(mz_send.at[h], mz_recv.at[h], to_zl, mz_recv.at[h])
 
-    spread_t[1].forward()
     ring_m.finish()
     mz_waits = [m_swap(0)]
     mown[0, 0], mown[0, 1] = moments(zl, 0)

time: 131 us -> 130 us (level)
  no operation moved by 1% of the time
where the time goes in v4:
time: 130 us
  Pallas kernels  129 us (99%)
    pallas_call x1, Pallas kernels, body(): pl.pallas_call(kernel, out_shape=(out, out, out), in_specs=[vmem, vmem, v...  126 us

profile of v4, /device:TPU:0, one launch (start us, length us, event | category | flops | bytes accessed | tf_op | source)
XLA Modules:
  0.0 129.7 jit_solution(10602478536423657276)
XLA Ops:
  0.6 126.5 %shard_map.112 = (f32[256,512]{1,0:T(8,128)}, f32[256,512]{1,0:T(8,128)}, f32[256,512]{1,0:T(8,128)}) custom-call(bf16[256,512]{1,0:T(8,128)(2,1)} %grad.1, f32[256,512]{1,0:T(8,128)} %m1.1, f32[256,512]{1,0:T(8,128)} %m2.1, s32[256,4096]{1,0:T(8,128)} %l_codes.1, f32[32,256]{1,0:T(8,128)} %bitcast.5, s32[512,4096]{1,0:T(8,128)} %o_codes.1, ...), custom_call_target="tpu_custom_call" | custom-call | tf_op jit(solution)/shard_map/pallas_call | solution.py:492
  127.1 2.5 %shard_map.113 = (f32[256,512]{1,0:T(8,128)}, f32[256,512]{1,0:T(8,128)}, f32[256,512]{1,0:T(8,128)}) custom-call(f32[256,512]{1,0:T(8,128)} %get-tuple-element.6.refs_0_, f32[256,512]{1,0:T(8,128)} %get-tuple-element.7.refs_1_, f32[256,512]{1,0:T(8,128)} %get-tuple-element.8.refs_2_), custom_call_target="tpu_custom_call" | custom-call | tf_op jit(solution)/shard_map/pallas_call | solution.py:505
